TPU v7x, 32 devices: a whole 2x2x4 slice. The times are simulated.
32 devices in a mesh: grp: 4 (over z), seq: 8 (over y, x, core).
Axes of the slice: x: 2, y: 2, z: 4, core: 2. Of those that a mesh axis runs over, the one named last changes fastest.
Arguments:
- signal: bfloat16 [8192, 256], P(('grp', 'seq')), may hold values from -6 to 6
- cotangent: bfloat16 [8192, 256], P(('grp', 'seq')), may hold values from -6 to 6
- w_taps: bfloat16 [512, 1024], replicated, may hold values from -0.25 to 0.25
- gate_bias: float32 [1024], replicated, may hold values from -3 to 3
- w_out: bfloat16 [512, 256], replicated, may hold values from -0.25 to 0.25
Outputs:
- block_out: bfloat16 [8192, 256], P(('grp', 'seq'))
- grad_in: bfloat16 [8192, 256], P(('grp', 'seq'))
- grad_taps: float32 [512, 1024], P('seq')
- grad_bias: float32 [1024], P('seq')
- grad_out: float32 [512, 256], P('seq')
All inputs are finite; a program needn't handle non-finite values.
Results may differ from a plain program's by a relative error of at most 0.0045.
Values may be sent and summed in bfloat16 or wider, within the bound.
A program may use at most 64 MiB of HBM per device.

v0:
```python
import jax
import jax.numpy as jnp
from jax import lax
from jax.sharding import PartitionSpec as P


def from_behind(array, axis, by):
    count = lax.axis_size(axis)
    pairs = [(i, i + by) for i in range(count) if 0 <= i + by < count]
    return lax.ppermute(array, axis, pairs)


def reduced_row_axes(left, right):
    return lax.dot_general(
        left, right, (((0,), (0,)), ((), ())), preferred_element_type=jnp.float32
    )


def contract_cols(left, right):
    return lax.dot_general(
        left, right, (((1,), (1,)), ((), ())), preferred_element_type=jnp.float32
    )


def per_device(signal, cotangent, w_taps, gate_bias, w_out):
    width = signal.shape[1]
    units = w_out.shape[0]
    lagged_input = from_behind(signal, ("grp", "seq"), 2)
    preact = jnp.dot(signal, w_taps[width:], preferred_element_type=jnp.float32)
    preact = (
        preact
        + jnp.dot(lagged_input, w_taps[:width], preferred_element_type=jnp.float32)
        + gate_bias
    )
    squashed = jnp.tanh(preact[:, :units])
    opened = jax.nn.sigmoid(preact[:, units:])
    hidden_state = (squashed * opened).astype(jnp.bfloat16)
    block_out = (
        signal.astype(jnp.float32)
        + jnp.dot(hidden_state, w_out, preferred_element_type=jnp.float32)
    ).astype(jnp.bfloat16)
    grad_hidden = contract_cols(cotangent, w_out)
    grad_pre = jnp.concatenate(
        [
            grad_hidden * opened * (1.0 - squashed * squashed),
            grad_hidden * squashed * opened * (1.0 - opened),
        ],
        axis=1,
    ).astype(jnp.bfloat16)
    part_out = reduced_row_axes(hidden_state, cotangent)
    part_taps = jnp.concatenate(
        [reduced_row_axes(lagged_input, grad_pre), reduced_row_axes(signal, grad_pre)], axis=0
    )
    part_bias = jnp.sum(grad_pre.astype(jnp.float32), axis=0)
    later_pre = from_behind(grad_pre, ("grp", "seq"), -2)
    tapped_signal = contract_cols(later_pre, w_taps[:width])
    nearby = cotangent.astype(jnp.float32) + contract_cols(grad_pre, w_taps[width:])
    grad_in = (nearby + tapped_signal).astype(jnp.bfloat16)
    total_taps, total_bias, total_out = lax.psum((part_taps, part_bias, part_out), ("grp", "seq"))
    groups = lax.axis_size("seq")
    where = lax.axis_index("seq")
    share_taps = total_taps.shape[0] // groups
    share_bias = total_bias.shape[0] // groups
    share_out = total_out.shape[0] // groups
    grad_taps = lax.dynamic_slice_in_dim(total_taps, where * share_taps, share_taps, 0)
    grad_bias = lax.dynamic_slice_in_dim(total_bias, where * share_bias, share_bias, 0)
    grad_out = lax.dynamic_slice_in_dim(total_out, where * share_out, share_out, 0)
    return (block_out, grad_in, grad_taps, grad_bias, grad_out)


def solution(mesh):
    placed = (P(("grp", "seq"), None), P(("grp", "seq"), None), P(), P(), P())
    return jax.shard_map(
        per_device,
        mesh=mesh,
        in_specs=placed,
        out_specs=(
            P(("grp", "seq"), None),
            P(("grp", "seq"), None),
            P("seq", None),
            P("seq"),
            P("seq", None),
        ),
        check_vma=False,
    )
```

profile of v0, /device:TPU:0, one launch (start us, length us, event | category | flops | bytes accessed | tf_op | source)
XLA Modules:
  0.0 170.4 jit_solution(3916047432204245733)
XLA Ops:
  7.2 0.0 copy-start
  7.2 0.0 copy-start.3
  7.2 0.0 all-reduce.3.cloned.1.call-start
  7.2 5.0 %collective-permute-start = (bf16[256,256]{1,0:T(8,128)(2,1)}, bf16[256,256]{1,0:T(8,128)(2,1)S(1)}, u32[]{:S(2)}, u32[]{:S(2)}) collective-permute-start(bf16[256,256]{1,0:T(8,128)(2,1)} %param.5), channel_id=1, source_target_pairs={{0,2},{1,3},{2,4},{3,5},{4,6},{5,7},{6,8},{7,9},{8,10},{9,11},{10,... | collective-permute-start | bytes 393224 | tf_op jit(solution)/shard_map/ppermute | solution.py:10
  12.2 1.4 fusion.9
  13.7 1.6 collective-permute-done
  15.3 1.3 fusion
  16.6 0.0 copy-done
  16.6 0.0 copy-done.3
  16.6 0.0 copy-start.2
  16.7 0.4 multiply_convert_fusion.1
  17.1 1.1 fusion.11
  18.2 0.0 copy-done.2
  18.2 0.3 convolution_bitcast_fusion
  18.5 0.3 convolution_bitcast_fusion.1
  18.9 1.4 pad_maximum_fusion
  20.3 0.0 copy-start.1
  20.3 0.0 all-reduce.3.cloned.1.call-update
  20.4 0.1 pad_maximum_fusion.1
  20.4 1.4 collective-permute-start.1
  21.9 0.1 convert_reduce_fusion
  22.0 53.8 %psum.22 = f32[1024]{0:T(1024)S(1)} all-reduce(f32[1024]{0:T(1024)S(1)} %convert_reduce_fusion), channel_id=1, replica_groups=mesh['grp'=4,'seq'=8] {'grp','seq'}, use_global_device_ids=true, to_apply=%region_2.0 | all-reduce | flops 1024 | bytes 8192 | tf_op jit(solution)/shard_map/psum | solution.py:59
  75.8 0.6 dynamic_slice.10
  76.4 0.9 fusion.1
  77.3 0.0 copy-done.1
  77.3 0.3 convolution_add_fusion.3
  77.6 0.0 collective-permute-done.1
  77.6 1.0 fusion.2
  78.6 81.8 %all-reduce.3.cloned.1.call-done = (f32[512,1024]{1,0:T(8,128)}, f32[512,256]{1,0:T(8,128)}) async-done(((f32[512,1024]{1,0:T(8,128)}, f32[512,256]{1,0:T(8,128)}), (f32[512,1024]{1,0:T(8,128)}, f32[512,256]{1,0:T(8,128)})) %all-reduce.3.cloned.1.call-update) | async-done | bytes 2621456 | tf_op jit(solution)/shard_map/psum | solution.py:59
  160.4 1.7 constant_dynamic-slice_fusion.1
  162.1 1.5 constant_dynamic-slice_fusion
Async XLA Ops:
  7.2 9.5 %copy-start = (bf16[512,256]{1,0:T(8,128)(2,1)S(1)}, bf16[512,256]{1,0:T(8,128)(2,1)}, u32[]{:S(2)}) copy-start(bf16[512,256]{1,0:T(8,128)(2,1)} %param.9) | copy-start | bytes 786436
  7.2 9.5 %copy-start.3 = (bf16[256,256]{1,0:T(8,128)(2,1)S(1)}, bf16[256,256]{1,0:T(8,128)(2,1)}, u32[]{:S(2)}) copy-start(bf16[256,256]{1,0:T(8,128)(2,1)} %param.6) | copy-start | bytes 393220
  7.2 153.2 %all-reduce.3.cloned.1.call-start = ((), (), s32[]{:S(2)}) async-start(), calls=%async_computation | async-start | bytes 5242880 | tf_op jit(solution)/shard_map/psum | solution.py:59
  7.2 8.0 %collective-permute-start = (bf16[256,256]{1,0:T(8,128)(2,1)}, bf16[256,256]{1,0:T(8,128)(2,1)S(1)}, u32[]{:S(2)}, u32[]{:S(2)}) collective-permute-start(bf16[256,256]{1,0:T(8,128)(2,1)} %param.5), channel_id=1, source_target_pairs={{0,2},{1,3},{2,4},{3,5},{4,6},{5,7},{6,8},{7,9},{8,10},{9,11},{10,... | collective-permute-start | bytes 393224 | tf_op jit(solution)/shard_map/ppermute | solution.py:10
  16.6 1.6 copy-start.2
  20.3 56.9 %copy-start.1 = (bf16[512,1024]{1,0:T(8,128)(2,1)S(1)}, bf16[512,1024]{1,0:T(8,128)(2,1)}, u32[]{:S(2)}) copy-start(bf16[512,1024]{1,0:T(8,128)(2,1)} %param.7) | copy-start | bytes 3145732
  20.4 57.2 %collective-permute-start.1 = (bf16[256,1024]{1,0:T(8,128)(2,1)S(1)}, bf16[256,1024]{1,0:T(8,128)(2,1)S(1)}, u32[]{:S(2)}, u32[]{:S(2)}) collective-permute-start(bf16[256,1024]{1,0:T(8,128)(2,1)S(1)} %pad_maximum_fusion.1), channel_id=1, source_target_pairs={{2,0},{3,1},{4,2},{5,3},{6,4},{7,5},{8,6},{9,7},{10,8},{11,9},{12,... | collective-permute-start | bytes 1572872 | tf_op jit(solution)/shard_map/ppermute | solution.py:10
Sparse Core Ops, SparseCore 0:
  20.5 139.8 all-reduce.2
where the time goes:
time: 171 us; the launch traced here: 170 us
  waiting for transfers between devices  83.4 us (49%)
  blocking collectives  53.8 us (31%)
  between operations  14.1 us (8%)
  matrix products  7.2 us (4%)
  starting transfers between devices  6.44 us (4%)
  local copies, waits for them, and re-layouts  3.75 us (2%)
    psum x1, waiting for transfers between devices, per_device(): lax.psum((part_taps, part_bias, part_out), ('grp', 'seq'))  81.8 us
    psum x1, blocking collectives, per_device(): lax.psum((part_taps, part_bias, part_out), ('grp', 'seq'))  53.8 us
    ppermute x2, starting transfers between devices, from_behind(): return lax.ppermute(array, axis, pairs)  6.41 us
  transfers between devices with their start and end apart: 3, of which 2 were waited for; matrix products, arithmetic and copies ran while one was open for 3% of the time, Pallas kernels for 0%

commit v1 on v0

v1 whole, which is shorter than its diff:
```python
import functools

import jax
import jax.numpy as jnp
from jax import lax
from jax.experimental import pallas as pl
from jax.experimental.pallas import tpu as pltpu
from jax.sharding import PartitionSpec as P

MESH = pl.DeviceIdType.MESH
F32 = jnp.float32
BF16 = jnp.bfloat16
UNIT_BLOCK = 256
LAG = 2


def dot(left, right, dims=((1,), (0,))):
    return lax.dot_general(left, right, (dims, ((), ())), preferred_element_type=F32)


def kernel(cfg, sig_ref, cot_ref, wt_ref, bias_ref, wo_ref, block_ref, gin_ref, taps_ref, gb_ref, gout_ref, *scratch):
    S, G, C, R, widths, split, bias_inside = cfg
    NP = len(widths)
    it = iter(scratch)
    take = lambda: next(it)
    lag, pre, gh, gp, hid, tap_s, tap_r = [take() for _ in range(7)]
    part = [take() for _ in range(NP)]
    core_r = [take() for _ in range(NP)]
    xs = [take() for _ in range(NP)]
    xr = [take() for _ in range(NP)]
    tot = [take() for _ in range(NP)]
    zs = [take() for _ in range(NP)]
    zr = [take() for _ in range(NP)]
    ag = [take() for _ in range(NP)]
    b0, b_core, b1, b_x, b2, b_z = [take() for _ in range(6)]
    halo_ss, halo_rs, core_ss, core_rs, x_ss, x_rs, z_ss, z_rs, a_ss, a_rs = [take() for _ in range(10)]
    BP = NP

    width = sig_ref.shape[1]
    units = wo_ref.shape[0]
    U = UNIT_BLOCK
    NB = units // U

    g = lax.axis_index("grp")
    s = lax.axis_index("seq")
    c = lax.rem(s, 2)
    q = s // 2
    flat = g * S + s
    has_prev = flat >= LAG
    has_next = flat < S * G - LAG
    nxt = lax.rem(flat + LAG, S * G)
    prv = lax.rem(flat + S * G - LAG, S * G)
    nxt_id = (nxt // S, lax.rem(nxt, S))
    prv_id = (prv // S, lax.rem(prv, S))
    other = (g, 2 * q + 1 - c)
    x_to = [(g, 2 * lax.rem(q + k, C) + c) for k in range(1, C)]
    z_to = [(lax.rem(g + k, G), s) for k in range(1, G)]

    barrier = pltpu.get_barrier_semaphore()
    for dev in [nxt_id, prv_id, other] + x_to + z_to:
        pl.semaphore_signal(barrier, inc=1, device_id=dev, device_id_type=MESH)
    pl.semaphore_wait(barrier, 3 + (C - 1) + (G - 1))

    def remote(src, dst, ss, rs, dev):
        return pltpu.make_async_remote_copy(
            src_ref=src, dst_ref=dst, send_sem=ss, recv_sem=rs, device_id=dev, device_id_type=MESH
        )

    halo = remote(sig_ref, lag, halo_ss.at[0], halo_rs.at[0], nxt_id)
    back = remote(tap_s, tap_r, halo_ss.at[1], halo_rs.at[1], prv_id)

    @pl.when(has_next)
    def _():
        halo.start()

    sig = sig_ref[...]
    pre[...] = dot(sig, wt_ref[width:, :]) + bias_ref[...]
    gh[...] = dot(cot_ref[...], wo_ref[...], ((1,), (1,)))

    @pl.when(has_prev)
    def _():
        halo.wait_recv()

    @pl.when(jnp.logical_not(has_prev))
    def _():
        lag[...] = jnp.zeros_like(lag)

    def core_copy(p):
        if p == BP:
            return remote(b0, b_core, core_ss.at[p], core_rs.at[p], other)
        return remote(part[p].at[1 - c], core_r[p], core_ss.at[p], core_rs.at[p], other)

    def x_copies(p):
        src, dst = (b1, b_x) if p == BP else (xs[p], xr[p])
        return [
            remote(
                src if p == BP else src.at[k],
                dst.at[k],
                x_ss.at[p, k],
                x_rs.at[p, k],
                x_to[k],
            )
            for k in range(C - 1)
        ]

    def z_copies(p):
        out = []
        for k in range(G - 1):
            to = lax.rem(g + k + 1, G)
            if p == BP:
                src, dst = b2, b_z.at[g]
            elif split:
                src, dst = zs[p].at[to], zr[p].at[k]
            else:
                src, dst = zs[p], zr[p].at[g]
            out.append(remote(src, dst, z_ss.at[p, k], z_rs.at[p, k], z_to[k]))
        return out

    def z_wait_recv(p):
        for k in range(G - 1):
            frm = lax.rem(g + G - k - 1, G)
            if p == BP:
                src, dst = b2, b_z.at[frm]
            elif split:
                src, dst = zs[p].at[frm], zr[p].at[k]
            else:
                src, dst = zs[p], zr[p].at[frm]
            remote(src, dst, z_ss.at[p, k], z_rs.at[p, k], z_to[k]).wait_recv()

    def a_copies(p):
        return [
            remote(ag[p].at[g], ag[p].at[g], a_ss.at[p, k], a_rs.at[p, k], z_to[k])
            for k in range(G - 1)
        ]

    def store_part(p, acc, base):
        for j in range(acc.shape[0] // R):
            n = base // R + j
            part[p][n % 2, n // 2] = acc[j * R : (j + 1) * R]

    def put(p, value):
        if p == NP - 1:
            gout_ref[...] = value
        else:
            taps_ref[:, p * U : (p + 1) * U] = value[:, :U]
            taps_ref[:, units + p * U : units + (p + 1) * U] = value[:, U:]

    def stage0(p):
        if p < NB:
            f_cols = slice(p * U, (p + 1) * U)
            g_cols = slice(units + p * U, units + (p + 1) * U)
            lagged = lag[...]
            filt = pre[:, f_cols] + dot(lagged, wt_ref[:width, f_cols])
            gate = pre[:, g_cols] + dot(lagged, wt_ref[:width, g_cols])
            t = jnp.tanh(filt)
            o = 0.5 * jnp.tanh(0.5 * gate) + 0.5
            hid[:, f_cols] = (t * o).astype(BF16)
            go = gh[:, f_cols] * o
            gp[:, f_cols] = (go * (1.0 - t * t)).astype(BF16)
            gp[:, g_cols] = (go * t * (1.0 - o)).astype(BF16)
            both = jnp.concatenate([gp[:, f_cols], gp[:, g_cols]], axis=1)
            store_part(p, dot(lagged, both, ((0,), (0,))), 0)
            store_part(p, dot(sig_ref[...], both, ((0,), (0,))), width)
        elif p == NB:
            store_part(p, dot(hid[...], cot_ref[...], ((0,), (0,))), 0)
        else:
            ones = jnp.ones((8, gp.shape[0]), BF16)
            b0[...] = dot(ones, gp[...])[0:1]
        core_copy(p).start()

    def stage1(p):
        core_copy(p).wait_recv()
        if p == BP:
            b1[...] = b0[...] + b_core[...]
        else:
            for k in range(C - 1):
                chip = lax.rem(q + k + 1, C)
                xs[p][k] = (part[p][c, chip] + core_r[p][chip]).astype(BF16)
        for copy in x_copies(p):
            copy.start()

    def stage2(p):
        for copy in x_copies(p):
            copy.wait_recv()
        if p == BP:
            total = b1[...]
            for k in range(C - 1):
                total = total + b_x[k]
            b2[...] = total
            b_z[g] = total
        else:
            total = part[p][c, q] + core_r[p][q]
            for k in range(C - 1):
                total = total + xr[p][k].astype(F32)
            if split:
                rows = R // G
                for j in range(G):
                    tot[p][j] = total[j * rows : (j + 1) * rows]
                    zs[p][j] = total[j * rows : (j + 1) * rows].astype(BF16)
            else:
                zs[p][...] = total.astype(BF16)
                zr[p][g] = total.astype(BF16)
        for copy in z_copies(p):
            copy.start()

    def stage3(p):
        z_wait_recv(p)
        if p == BP:
            total = b_z[0]
            for k in range(1, G):
                total = total + b_z[k]
            if bias_inside:
                share = gb_ref.shape[1]
                mine = total[:, :share]
                for j in range(1, S):
                    mine = jnp.where(s == j, total[:, j * share : (j + 1) * share], mine)
                gb_ref[...] = mine
            else:
                gb_ref[...] = total
        elif split:
            total = tot[p][g]
            for k in range(G - 1):
                total = total + zr[p][k].astype(F32)
            ag[p][g] = total.astype(BF16)
            for copy in a_copies(p):
                copy.start()
        else:
            total = zr[p][0].astype(F32)
            for k in range(1, G):
                total = total + zr[p][k].astype(F32)
            put(p, total)

    def stage4(p):
        if p == BP or not split:
            return
        for k in range(G - 1):
            frm = lax.rem(g + G - k - 1, G)
            remote(ag[p].at[g], ag[p].at[frm], a_ss.at[p, k], a_rs.at[p, k], z_to[k]).wait_recv()
        value = jnp.concatenate([ag[p][j].astype(F32) for j in range(G)], axis=0)
        put(p, value)

    for p in range(NB):
        stage0(p)
        if p > 0:
            stage1(p - 1)

    tap_s[...] = dot(gp[...], wt_ref[:width, :], ((1,), (1,))).astype(BF16)

    @pl.when(has_prev)
    def _():
        back.start()

    stage0(NB)
    stage1(NB - 1)
    stage0(BP)
    stage1(NB)
    stage1(BP)

    block_ref[...] = (sig_ref[...].astype(F32) + dot(hid[...], wo_ref[...])).astype(BF16)
    nearby = cot_ref[...].astype(F32) + dot(gp[...], wt_ref[width:, :], ((1,), (1,)))

    @pl.when(has_next)
    def _():
        back.wait_recv()

    @pl.when(jnp.logical_not(has_next))
    def _():
        tap_r[...] = jnp.zeros_like(tap_r)

    gin_ref[...] = (nearby + tap_r[...].astype(F32)).astype(BF16)

    for p in range(NP + 1 + 2):
        if p <= BP:
            stage2(p)
        if 0 <= p - 1 <= BP:
            stage3(p - 1)
        if 0 <= p - 2 <= BP:
            stage4(p - 2)

    @pl.when(has_next)
    def _():
        halo.wait_send()

    @pl.when(has_prev)
    def _():
        back.wait_send()

    for p in range(NP + 1):
        core_copy(p).wait_send()
        for copy in x_copies(p):
            copy.wait_send()
        for copy in z_copies(p):
            copy.wait_send()
        if p < NP and split:
            for copy in a_copies(p):
                copy.wait_send()


def per_device(S, G, signal, cotangent, w_taps, gate_bias, w_out):
    steps, width = signal.shape
    units = w_out.shape[0]
    C = S // 2
    R = 2 * width // S
    U = UNIT_BLOCK
    NB = units // U
    widths = [2 * U] * NB + [width]
    NP = len(widths)
    split = R % (16 * G) == 0
    share = 2 * units // S
    bias_inside = share % 128 == 0
    zrows = R // G if split else R
    V = pltpu.VMEM
    D = pltpu.SemaphoreType.DMA
    scratch = [
        V((steps, width), BF16),
        V((steps, 2 * units), F32),
        V((steps, units), F32),
        V((steps, 2 * units), BF16),
        V((steps, units), BF16),
        V((steps, width), BF16),
        V((steps, width), BF16),
    ]
    scratch += [V((2, C, R, w), F32) for w in widths]
    scratch += [V((C, R, w), F32) for w in widths]
    scratch += [V((C - 1, R, w), BF16) for w in widths]
    scratch += [V((C - 1, R, w), BF16) for w in widths]
    scratch += [V((G, zrows, w) if split else (8, 128), F32) for w in widths]
    scratch += [V((G, zrows, w) if split else (zrows, w), BF16) for w in widths]
    scratch += [V((G - 1 if split else G, zrows, w), BF16) for w in widths]
    scratch += [V((G, zrows, w) if split else (16, 128), BF16) for w in widths]
    one = (1, 2 * units)
    scratch += [V(one, F32), V(one, F32), V(one, F32), V((C - 1,) + one, F32), V(one, F32), V((G,) + one, F32)]
    scratch += [
        D((2,)), D((2,)),
        D((NP + 1,)), D((NP + 1,)),
        D((NP + 1, C - 1)), D((NP + 1, C - 1)),
        D((NP + 1, G - 1)), D((NP + 1, G - 1)),
        D((NP, G - 1)), D((NP, G - 1)),
    ]
    vmem = pl.BlockSpec(memory_space=pltpu.VMEM)
    outs = pl.pallas_call(
        functools.partial(kernel, (S, G, C, R, tuple(widths), split, bias_inside)),
        out_shape=(
            jax.ShapeDtypeStruct((steps, width), BF16),
            jax.ShapeDtypeStruct((steps, width), BF16),
            jax.ShapeDtypeStruct((R, 2 * units), F32),
            jax.ShapeDtypeStruct((1, share if bias_inside else 2 * units), F32),
            jax.ShapeDtypeStruct((units // S, width), F32),
        ),
        in_specs=[vmem] * 5,
        out_specs=[vmem] * 5,
        scratch_shapes=scratch,
        compiler_params=pltpu.CompilerParams(
            collective_id=0, has_side_effects=True, vmem_limit_bytes=48 * 1024 * 1024
        ),
        cost_estimate=pl.CostEstimate(
            flops=2 * steps * width * units * 16, bytes_accessed=4 << 20, transcendentals=2 * steps * units
        ),
    )(signal, cotangent, w_taps, gate_bias.reshape(1, -1), w_out)
    block_out, grad_in, grad_taps, grad_bias, grad_out = outs
    grad_bias = grad_bias.reshape(-1)
    if not bias_inside:
        grad_bias = lax.dynamic_slice_in_dim(grad_bias, lax.axis_index("seq") * share, share, 0)
    return block_out, grad_in, grad_taps, grad_bias, grad_out


def solution(mesh):
    S, G = mesh.shape["seq"], mesh.shape["grp"]
    rows = P(("grp", "seq"), None)
    return jax.shard_map(
        functools.partial(per_device, S, G),
        mesh=mesh,
        in_specs=(rows, rows, P(), P(), P()),
        out_specs=(rows, rows, P("seq", None), P("seq"), P("seq", None)),
        check_vma=False,
    )
```

time: 171 us -> 42 us (0.25)
  waiting for transfers between devices: 83.4 us -> 0 us
  blocking collectives: 53.8 us -> 0 us
  Pallas kernels: 0 us -> 33.3 us
  between operations: 14.1 us -> 0.66 us
  matrix products: 7.2 us -> 0 us
  starting transfers between devices: 6.44 us -> 0 us
  local copies, waits for them, and re-layouts: 3.75 us -> 7.82 us
    psum x1 -> x0, waiting for transfers between devices: 81.8 us -> none  [per_device(): lax.psum((part_taps, part_bias, part_out), ('grp', 'seq'))]
    psum x1 -> x0, blocking collectives: 53.8 us -> none  [per_device(): lax.psum((part_taps, part_bias, part_out), ('grp', 'seq'))]
    pallas_call x0 -> x1, Pallas kernels: none -> 33.3 us  [per_device(): pl.pallas_call(functools.partial(kernel, (S, G, C, R, tuple(widths), spli...]
    unnamed x8 -> x15, local copies, waits for them, and re-layouts: 0.02 us -> 7.82 us
    dot_general x9 -> x0, matrix products: 7.2 us -> none  [the longest x3 1.79 us: contract_cols(): lax.dot_general(left, right, (((1,), (1,)), ((), ())), preferred_element_...]
    ppermute x2 -> x0, starting transfers between devices: 6.41 us -> none  [from_behind(): return lax.ppermute(array, axis, pairs)]
    dynamic_slice x3 -> x0, local copies, waits for them, and re-layouts: 3.72 us -> none  [the longest x1 1.67 us: per_device(): lax.dynamic_slice_in_dim(total_taps, where * share_taps, share_taps, 0)]
  transfers between devices with their start and end apart: 3 -> 0, of which waited for: 2 -> 0; matrix products, arithmetic and copies ran while one was open for 3% -> 0% of each run, Pallas kernels for 0% -> 0%
where the time goes in v1:
time: 42 us; the launch traced here: 41.7 us
  Pallas kernels  33.3 us (79%)
  local copies, waits for them, and re-layouts  7.82 us (19%)
  between operations  0.66 us (2%)
    pallas_call x1, Pallas kernels, per_device(): pl.pallas_call(functools.partial(kernel, (S, G, C, R, tuple(widths), spli...  33.3 us
    unnamed x15, local copies, waits for them, and re-layouts  7.82 us

profile of v1, /device:TPU:0, one launch (start us, length us, event | category | flops | bytes accessed | tf_op | source)
XLA Modules:
  0.0 41.7 jit_solution(17888991532587934201)
XLA Ops:
  0.6 0.0 copy-start
  0.6 1.2 %copy-done = bf16[512,1024]{1,0:T(8,128)(2,1)S(1)} copy-done((bf16[512,1024]{1,0:T(8,128)(2,1)S(1)}, bf16[512,1024]{1,0:T(8,128)(2,1)}, u32[]{:S(2)}) %copy-start) | copy-done | bytes 1048600
  1.9 0.0 copy-start.1
  1.9 0.9 %copy-done.1 = bf16[512,256]{1,0:T(8,128)(2,1)S(1)} copy-done((bf16[512,256]{1,0:T(8,128)(2,1)S(1)}, bf16[512,256]{1,0:T(8,128)(2,1)}, u32[]{:S(2)}) %copy-start.1) | copy-done | bytes 262168
  2.8 0.0 copy-start.2
  2.8 0.9 %copy-done.2 = bf16[256,256]{1,0:T(8,128)(2,1)S(1)} copy-done((bf16[256,256]{1,0:T(8,128)(2,1)S(1)}, bf16[256,256]{1,0:T(8,128)(2,1)}, u32[]{:S(2)}) %copy-start.2) | copy-done | bytes 131096
  3.7 0.0 copy-start.3
  3.7 0.9 %copy-done.3 = bf16[256,256]{1,0:T(8,128)(2,1)S(1)} copy-done((bf16[256,256]{1,0:T(8,128)(2,1)S(1)}, bf16[256,256]{1,0:T(8,128)(2,1)}, u32[]{:S(2)}) %copy-start.3) | copy-done | bytes 131096
  4.6 0.0 copy-start.4
  4.6 0.7 %copy-done.4 = f32[1024]{0:T(1024)S(1)} copy-done((f32[1024]{0:T(1024)S(1)}, f32[1024]{0:T(1024)}, u32[]{:S(2)}) %copy-start.4) | copy-done | bytes 4120
  5.3 33.3 %shard_map.92 = (bf16[256,256]{1,0:T(8,128)(2,1)S(1)}, bf16[256,256]{1,0:T(8,128)(2,1)S(1)}, f32[64,1024]{1,0:T(8,128)S(1)}, f32[1,128]{1,0:T(1,128)S(1)}, f32[64,256]{1,0:T(8,128)S(1)}) custom-call(bf16[256,256]{1,0:T(8,128)(2,1)S(1)} %copy-done.2, bf16[256,256]{1,0:T(8,128)(2,1)S(1)} %copy-done.3, bf16[512,1024]{1,0:T(8,128)(2,1)S(1)} %copy-done, ...), custom_call_target="tpu_custom_call" | custom-call | flops 1073741824 | bytes 4194304 | tf_op jit(solution)/shard_map/pallas_call | solution.py:341
  38.6 0.7 %copy.15 = bf16[256,256]{1,0:T(8,128)(2,1)} copy(bf16[256,256]{1,0:T(8,128)(2,1)S(1)} %get-tuple-element.20) | data formatting | bytes 262144
  39.3 0.7 %copy.16 = bf16[256,256]{1,0:T(8,128)(2,1)} copy(bf16[256,256]{1,0:T(8,128)(2,1)S(1)} %get-tuple-element.21) | data formatting | bytes 262144
  39.9 0.7 %copy.17 = f32[64,1024]{1,0:T(8,128)} copy(f32[64,1024]{1,0:T(8,128)S(1)} %get-tuple-element.22) | data formatting | bytes 524288
  40.6 0.5 %copy.18 = f32[128]{0:T(128)} copy(f32[128]{0:T(128)S(1)} %bitcast.3) | data formatting | bytes 1024
  41.1 0.6 %copy.19 = f32[64,256]{1,0:T(8,128)} copy(f32[64,256]{1,0:T(8,128)S(1)} %get-tuple-element.24) | data formatting | bytes 131072
Async XLA Ops:
  0.6 1.2 %copy-start = (bf16[512,1024]{1,0:T(8,128)(2,1)S(1)}, bf16[512,1024]{1,0:T(8,128)(2,1)}, u32[]{:S(2)}) copy-start(bf16[512,1024]{1,0:T(8,128)(2,1)} %wt_ref.1) | copy-start | bytes 3145732
  1.9 0.9 %copy-start.1 = (bf16[512,256]{1,0:T(8,128)(2,1)S(1)}, bf16[512,256]{1,0:T(8,128)(2,1)}, u32[]{:S(2)}) copy-start(bf16[512,256]{1,0:T(8,128)(2,1)} %wo_ref.1) | copy-start | bytes 786436
  2.8 0.9 %copy-start.2 = (bf16[256,256]{1,0:T(8,128)(2,1)S(1)}, bf16[256,256]{1,0:T(8,128)(2,1)}, u32[]{:S(2)}) copy-start(bf16[256,256]{1,0:T(8,128)(2,1)} %sig_ref.1) | copy-start | bytes 393220
  3.7 0.9 %copy-start.3 = (bf16[256,256]{1,0:T(8,128)(2,1)S(1)}, bf16[256,256]{1,0:T(8,128)(2,1)}, u32[]{:S(2)}) copy-start(bf16[256,256]{1,0:T(8,128)(2,1)} %cot_ref.1) | copy-start | bytes 393220
  4.6 0.7 %copy-start.4 = (f32[1024]{0:T(1024)S(1)}, f32[1024]{0:T(1024)}, u32[]{:S(2)}) copy-start(f32[1024]{0:T(1024)} %param.8) | copy-start | bytes 12292

commit v2 on v1

--- a/solution.py
+++ b/solution.py
@@ -18,11 +18,14 @@
     return lax.dot_general(left, right, (dims, ((), ())), preferred_element_type=F32)
 
 
-def kernel(cfg, sig_ref, cot_ref, wt_ref, bias_ref, wo_ref, block_ref, gin_ref, taps_ref, gb_ref, gout_ref, *scratch):
+def kernel(cfg, sig_in, cot_in, wt_in, bias_in, wo_in, *rest):
+    results, scratch = rest[:5], rest[5:]
     S, G, C, R, widths, split, bias_inside = cfg
     NP = len(widths)
     it = iter(scratch)
     take = lambda: next(it)
+    sig_ref, cot_ref, wt_ref, bias_ref, wo_ref, in_sem = [take() for _ in range(6)]
+    block_ref, gin_ref, taps_ref, gb_ref, gout_ref, out_sem, near = [take() for _ in range(7)]
     lag, pre, gh, gp, hid, tap_s, tap_r = [take() for _ in range(7)]
     part = [take() for _ in range(NP)]
     core_r = [take() for _ in range(NP)]
@@ -56,6 +59,14 @@
     x_to = [(g, 2 * lax.rem(q + k, C) + c) for k in range(1, C)]
     z_to = [(lax.rem(g + k, G), s) for k in range(1, G)]
 
+    loads = [
+        pltpu.make_async_copy(src, dst, in_sem.at[k])
+        for k, (src, dst) in enumerate(
+            [(sig_in, sig_ref), (wt_in, wt_ref), (bias_in, bias_ref), (cot_in, cot_ref), (wo_in, wo_ref)]
+        )
+    ]
+    for load in loads:
+        load.start()
     barrier = pltpu.get_barrier_semaphore()
     for dev in [nxt_id, prv_id, other] + x_to + z_to:
         pl.semaphore_signal(barrier, inc=1, device_id=dev, device_id_type=MESH)
@@ -66,15 +77,18 @@
             src_ref=src, dst_ref=dst, send_sem=ss, recv_sem=rs, device_id=dev, device_id_type=MESH
         )
 
-    halo = remote(sig_ref, lag, halo_ss.at[0], halo_rs.at[0], nxt_id)
+    halo = remote(sig_in, lag, halo_ss.at[0], halo_rs.at[0], nxt_id)
     back = remote(tap_s, tap_r, halo_ss.at[1], halo_rs.at[1], prv_id)
 
     @pl.when(has_next)
     def _():
         halo.start()
 
-    sig = sig_ref[...]
-    pre[...] = dot(sig, wt_ref[width:, :]) + bias_ref[...]
+    for load in loads[:3]:
+        load.wait()
+    pre[...] = dot(sig_ref[...], wt_ref[width:, :]) + bias_ref[...]
+    for load in loads[3:]:
+        load.wait()
     gh[...] = dot(cot_ref[...], wo_ref[...], ((1,), (1,)))
 
     @pl.when(has_prev)
@@ -239,25 +253,50 @@
         value = jnp.concatenate([ag[p][j].astype(F32) for j in range(G)], axis=0)
         put(p, value)
 
-    for p in range(NB):
+    stores = [
+        pltpu.make_async_copy(src, dst, out_sem.at[k])
+        for k, (src, dst) in enumerate(zip((block_ref, gin_ref, taps_ref, gb_ref, gout_ref), results))
+    ]
+
+    def sent(p):
+        for copy in x_copies(p):
+            copy.wait_send()
+
+    stage0(0)
+    for p in range(1, NB):
         stage0(p)
-        if p > 0:
-            stage1(p - 1)
-
+    stage1(0)
+    stage0(NB)
+    stage0(BP)
     tap_s[...] = dot(gp[...], wt_ref[:width, :], ((1,), (1,))).astype(BF16)
-
-    @pl.when(has_prev)
-    def _():
-        back.start()
-
-    stage0(NB)
-    stage1(NB - 1)
-    stage0(BP)
-    stage1(NB)
+    block_ref[...] = (sig_ref[...].astype(F32) + dot(hid[...], wo_ref[...])).astype(BF16)
+    stores[0].start()
+    near[...] = cot_ref[...].astype(F32) + dot(gp[...], wt_ref[width:, :], ((1,), (1,)))
     stage1(BP)
-
-    block_ref[...] = (sig_ref[...].astype(F32) + dot(hid[...], wo_ref[...])).astype(BF16)
-    nearby = cot_ref[...].astype(F32) + dot(gp[...], wt_ref[width:, :], ((1,), (1,)))
+    for step in range(1, NP + 3):
+        if step < NP:
+            sent(step - 1)
+            stage1(step)
+        if step == NP:
+            sent(NP - 1)
+
+            @pl.when(has_prev)
+            def _():
+                back.start()
+
+        if step == 2:
+            stage2(BP)
+        if step == 3:
+            stage3(BP)
+            stores[3].start()
+        if step - 1 < NP:
+            stage2(step - 1)
+        if 0 <= step - 2 < NP:
+            stage3(step - 2)
+        if 0 <= step - 3 < NP:
+            stage4(step - 3)
+            if step - 3 == NB - 1:
+                stores[2].start()
 
     @pl.when(has_next)
     def _():
@@ -267,15 +306,9 @@
     def _():
         tap_r[...] = jnp.zeros_like(tap_r)
 
-    gin_ref[...] = (nearby + tap_r[...].astype(F32)).astype(BF16)
-
-    for p in range(NP + 1 + 2):
-        if p <= BP:
-            stage2(p)
-        if 0 <= p - 1 <= BP:
-            stage3(p - 1)
-        if 0 <= p - 2 <= BP:
-            stage4(p - 2)
+    gin_ref[...] = (near[...] + tap_r[...].astype(F32)).astype(BF16)
+    stores[1].start()
+    stores[4].start()
 
     @pl.when(has_next)
     def _():
@@ -287,13 +320,24 @@
 
     for p in range(NP + 1):
         core_copy(p).wait_send()
-        for copy in x_copies(p):
-            copy.wait_send()
+        if p == BP:
+            sent(p)
         for copy in z_copies(p):
             copy.wait_send()
         if p < NP and split:
             for copy in a_copies(p):
                 copy.wait_send()
+    for store in stores:
+        store.wait()
+
+
+def write_out(*refs):
+    ins, outs, sem = refs[:5], refs[5:10], refs[10]
+    copies = [pltpu.make_async_copy(ins[k], outs[k], sem.at[k]) for k in range(5)]
+    for copy in copies:
+        copy.start()
+    for copy in copies:
+        copy.wait()
 
 
 def per_device(S, G, signal, cotangent, w_taps, gate_bias, w_out):
@@ -312,6 +356,19 @@
     V = pltpu.VMEM
     D = pltpu.SemaphoreType.DMA
     scratch = [
+        V((steps, width), BF16),
+        V((steps, width), BF16),
+        V((2 * width, 2 * units), BF16),
+        V((1, 2 * units), F32),
+        V((units, width), BF16),
+        D((5,)),
+        V((steps, width), BF16),
+        V((steps, width), BF16),
+        V((R, 2 * units), F32),
+        V((1, share if bias_inside else 2 * units), F32),
+        V((units // S, width), F32),
+        D((5,)),
+        V((steps, width), F32),
         V((steps, width), BF16),
         V((steps, 2 * units), F32),
         V((steps, units), F32),
@@ -347,17 +404,23 @@
             jax.ShapeDtypeStruct((1, share if bias_inside else 2 * units), F32),
             jax.ShapeDtypeStruct((units // S, width), F32),
         ),
-        in_specs=[vmem] * 5,
-        out_specs=[vmem] * 5,
+        in_specs=[pl.BlockSpec(memory_space=pltpu.HBM)] * 5,
+        out_specs=[pl.BlockSpec(memory_space=pltpu.HBM)] * 5,
         scratch_shapes=scratch,
         compiler_params=pltpu.CompilerParams(
-            collective_id=0, has_side_effects=True, vmem_limit_bytes=48 * 1024 * 1024
+            collective_id=0, has_side_effects=True, vmem_limit_bytes=64000 * 1024
         ),
         cost_estimate=pl.CostEstimate(
             flops=2 * steps * width * units * 16, bytes_accessed=4 << 20, transcendentals=2 * steps * units
         ),
     )(signal, cotangent, w_taps, gate_bias.reshape(1, -1), w_out)
-    block_out, grad_in, grad_taps, grad_bias, grad_out = outs
+    block_out, grad_in, grad_taps, grad_bias, grad_out = pl.pallas_call(
+        write_out,
+        out_shape=tuple(jax.ShapeDtypeStruct(o.shape, o.dtype) for o in outs),
+        in_specs=[vmem] * 5,
+        out_specs=[pl.BlockSpec(memory_space=pltpu.HBM)] * 5,
+        scratch_shapes=[D((5,))],
+    )(*outs)
     grad_bias = grad_bias.reshape(-1)
     if not bias_inside:
         grad_bias = lax.dynamic_slice_in_dim(grad_bias, lax.axis_index("seq") * share, share, 0)

time: 42 us -> 36.5 us (0.87)
  local copies, waits for them, and re-layouts: 7.82 us -> 0 us
  Pallas kernels: 33.3 us -> 35.7 us
    unnamed x15 -> x0, local copies, waits for them, and re-layouts: 7.82 us -> none
    pallas_call x0 -> x1, Pallas kernels: none -> 1.94 us  [per_device(): pl.pallas_call(write_out, out_shape=tuple((jax.ShapeDtypeStruct(o.shape,...]
    pallas_call x1, Pallas kernels: 33.3 us -> 33.7 us  [per_device(): pl.pallas_call(functools.partial(kernel, (S, G, C, R, tuple(widths), spli...]
where the time goes in v2:
time: 36.5 us; the launch traced here: 36.3 us
  Pallas kernels  35.7 us (98%)
  between operations  0.64 us (2%)
    pallas_call x1, Pallas kernels, per_device(): pl.pallas_call(functools.partial(kernel, (S, G, C, R, tuple(widths), spli...  33.7 us
    pallas_call x1, Pallas kernels, per_device(): pl.pallas_call(write_out, out_shape=tuple((jax.ShapeDtypeStruct(o.shape,...  1.94 us

profile of v2, /device:TPU:0, one launch (start us, length us, event | category | flops | bytes accessed | tf_op | source)
XLA Modules:
  0.0 36.3 jit_solution(6233539405847499546)
XLA Ops:
  0.6 33.7 %shard_map.92 = (bf16[256,256]{1,0:T(8,128)(2,1)}, bf16[256,256]{1,0:T(8,128)(2,1)}, f32[64,1024]{1,0:T(8,128)}, f32[1,128]{1,0:T(1,128)}, f32[64,256]{1,0:T(8,128)}) custom-call(bf16[256,256]{1,0:T(8,128)(2,1)} %sig_in.1, bf16[256,256]{1,0:T(8,128)(2,1)} %cot_in.1, bf16[512,1024]{1,0:T(8,128)(2,1)} %wt_in.1, f32[1,1024]{1,0:T(1,128)} %bitcast.2, ...), custom_call_target="tpu_custom_call" | custom-call | flops 1073741824 | bytes 4194304 | tf_op jit(solution)/shard_map/pallas_call | solution.py:398
  34.4 1.9 %shard_map.93 = (bf16[256,256]{1,0:T(8,128)(2,1)}, bf16[256,256]{1,0:T(8,128)(2,1)}, f32[64,1024]{1,0:T(8,128)}, f32[1,128]{1,0:T(1,128)}, f32[64,256]{1,0:T(8,128)}) custom-call(bf16[256,256]{1,0:T(8,128)(2,1)} %get-tuple-element.15.refs_0_, bf16[256,256]{1,0:T(8,128)(2,1)} %get-tuple-element.16.refs_1_, f32[64,1024]{1,0:T(8,128)} %get-tuple-element.17.refs_2_, ...), custom_call_target="tpu_custom_call" | custom-call | tf_op jit(solution)/shard_map/pallas_call | solution.py:417

commit v3 on v2

v3 whole, which is shorter than its diff:
```python
import functools

import jax
import jax.numpy as jnp
from jax import lax
from jax.experimental import pallas as pl
from jax.experimental.pallas import tpu as pltpu
from jax.sharding import PartitionSpec as P

MESH = pl.DeviceIdType.MESH
F32 = jnp.float32
BF16 = jnp.bfloat16
UNIT_BLOCK = 256
GROUPS = 3
LAYOUT = {(2, 3): ((0,), (1,), (2,)), (2, 2): ((0,), (1, 2)), (1, 2): ((0,), (1,)), (2, 1): ((0, 1, 2),), (1, 1): ((0, 1),)}
BIAS_LANES = 128
LAG = 2


def dot(left, right, dims=((1,), (0,))):
    return lax.dot_general(left, right, (dims, ((), ())), preferred_element_type=F32)


def kernel(cfg, sig_in, cot_in, wt_in, bias_in, wo_in, *rest):
    results, scratch = rest[:5], rest[5:]
    S, G, C, R, pieces, split = cfg
    NP = len(pieces)
    it = iter(scratch)
    take = lambda: next(it)
    sig_ref, cot_ref, wt_ref, bias_ref, wo_ref, in_sem = [take() for _ in range(6)]
    block_ref, gin_ref, taps_ref, gb_ref, gout_ref, out_sem, near = [take() for _ in range(7)]
    lag, pre, gh, gp, hid, tap_s, tap_r = [take() for _ in range(7)]
    part = [take() for _ in range(NP)]
    core_r = [take() for _ in range(NP)]
    xs = [take() for _ in range(NP)]
    xr = [take() for _ in range(NP)]
    tot = [take() for _ in range(NP)]
    zs = [take() for _ in range(NP)]
    zr = [take() for _ in range(NP)]
    ag = [take() for _ in range(NP)]
    halo_ss, halo_rs, core_ss, core_rs, x_ss, x_rs, z_ss, z_rs, a_ss, a_rs = [take() for _ in range(10)]

    width = sig_ref.shape[1]
    units = wo_ref.shape[0]
    U = UNIT_BLOCK
    NB = units // U

    g = lax.axis_index("grp")
    s = lax.axis_index("seq")
    c = lax.rem(s, 2)
    q = s // 2
    flat = g * S + s
    has_prev = flat >= LAG
    has_next = flat < S * G - LAG
    nxt = lax.rem(flat + LAG, S * G)
    prv = lax.rem(flat + S * G - LAG, S * G)
    nxt_id = (nxt // S, lax.rem(nxt, S))
    prv_id = (prv // S, lax.rem(prv, S))
    other = (g, 2 * q + 1 - c)
    x_to = [(g, 2 * lax.rem(q + k, C) + c) for k in range(1, C)]
    z_to = [(lax.rem(g + k, G), s) for k in range(1, G)]

    loads = [
        pltpu.make_async_copy(src, dst, in_sem.at[k])
        for k, (src, dst) in enumerate(
            [(sig_in, sig_ref), (wt_in, wt_ref), (bias_in, bias_ref), (cot_in, cot_ref), (wo_in, wo_ref)]
        )
    ]
    for load in loads:
        load.start()
    barrier = pltpu.get_barrier_semaphore()
    for dev in [nxt_id, prv_id, other] + x_to + z_to:
        pl.semaphore_signal(barrier, inc=1, device_id=dev, device_id_type=MESH)
    pl.semaphore_wait(barrier, 3 + (C - 1) + (G - 1))

    def remote(src, dst, ss, rs, dev):
        return pltpu.make_async_remote_copy(
            src_ref=src, dst_ref=dst, send_sem=ss, recv_sem=rs, device_id=dev, device_id_type=MESH
        )

    halo = remote(sig_in, lag, halo_ss.at[0], halo_rs.at[0], nxt_id)
    back = remote(tap_s, tap_r, halo_ss.at[1], halo_rs.at[1], prv_id)

    @pl.when(has_next)
    def _():
        halo.start()

    for load in loads[:3]:
        load.wait()
    pre[...] = dot(sig_ref[...], wt_ref[width:, :]) + bias_ref[...]
    for load in loads[3:]:
        load.wait()
    gh[...] = dot(cot_ref[...], wo_ref[...], ((1,), (1,)))

    @pl.when(has_prev)
    def _():
        halo.wait_recv()

    @pl.when(jnp.logical_not(has_prev))
    def _():
        lag[...] = jnp.zeros_like(lag)

    def core_copy(p):
        return remote(part[p].at[1 - c], core_r[p], core_ss.at[p], core_rs.at[p], other)

    def x_copies(p):
        return [
            remote(xs[p].at[k], xr[p].at[k], x_ss.at[p], x_rs.at[p], x_to[k])
            for k in range(C - 1)
        ]

    def x_all(p):
        return remote(xs[p], xr[p], x_ss.at[p], x_rs.at[p], other)

    def z_copies(p):
        out = []
        for k in range(G - 1):
            if split:
                src, dst = zs[p].at[lax.rem(g + k + 1, G)], zr[p].at[k]
            else:
                src, dst = zs[p], zr[p].at[k]
            out.append(remote(src, dst, z_ss.at[p], z_rs.at[p], z_to[k]))
        return out

    def z_all(p):
        return remote(zr[p], zr[p], z_ss.at[p], z_rs.at[p], other)

    def a_copies(p):
        return [
            remote(ag[p].at[g], ag[p].at[g], a_ss.at[p], a_rs.at[p], z_to[k]) for k in range(G - 1)
        ]

    def a_all(p):
        rest = ag[p].at[pl.ds(0, G - 1)]
        return remote(rest, rest, a_ss.at[p], a_rs.at[p], other)

    def store_part(p, col, acc, base):
        for j in range(acc.shape[0] // R):
            n = base // R + j
            part[p][n % 2, n // 2, :, col : col + acc.shape[1]] = acc[j * R : (j + 1) * R]

    def put(p, value):
        for block, col in pieces[p][0]:
            if block == NB:
                gout_ref[...] = value[:, col : col + width]
                share = gb_ref.shape[1]
                gb_ref[...] = value[0:1, col + width : col + width + share]
            else:
                taps_ref[:, block * U : (block + 1) * U] = value[:, col : col + U]
                taps_ref[:, units + block * U : units + (block + 1) * U] = value[:, col + U : col + 2 * U]

    def compute(p, block, col):
        if block < NB:
            b = block
            f_cols = slice(b * U, (b + 1) * U)
            g_cols = slice(units + b * U, units + (b + 1) * U)
            lagged = lag[...]
            filt = pre[:, f_cols] + dot(lagged, wt_ref[:width, f_cols])
            gate = pre[:, g_cols] + dot(lagged, wt_ref[:width, g_cols])
            t = jnp.tanh(filt)
            o = 0.5 * jnp.tanh(0.5 * gate) + 0.5
            hid[:, f_cols] = (t * o).astype(BF16)
            go = gh[:, f_cols] * o
            gp[:, f_cols] = (go * (1.0 - t * t)).astype(BF16)
            gp[:, g_cols] = (go * t * (1.0 - o)).astype(BF16)
            both = jnp.concatenate([gp[:, f_cols], gp[:, g_cols]], axis=1)
            store_part(p, col, dot(lagged, both, ((0,), (0,))), 0)
            store_part(p, col, dot(sig_ref[...], both, ((0,), (0,))), width)
        else:
            store_part(p, col, dot(hid[...], cot_ref[...], ((0,), (0,))), 0)
            ones = jnp.ones((8, gp.shape[0]), BF16)
            sums = dot(ones, gp[...])[0:1]
            part[p][:, :, :, col + width :] = jnp.zeros((2, C, R, BIAS_LANES), F32)
            share = gb_ref.shape[1]
            for n in range(S):
                part[p][n % 2, n // 2, 0:1, col + width : col + width + share] = sums[:, n * share : (n + 1) * share]

    def stage0(p):
        for block, col in pieces[p][0]:
            compute(p, block, col)
        core_copy(p).start()

    def stage1(p):
        core_copy(p).wait_recv()
        for k in range(C - 1):
            chip = lax.rem(q + k + 1, C)
            xs[p][k] = (part[p][c, chip] + core_r[p][chip]).astype(BF16)
        for copy in x_copies(p):
            copy.start()

    def stage2(p):
        total = part[p][c, q] + core_r[p][q]
        x_all(p).wait_recv()
        for k in range(C - 1):
            total = total + xr[p][k].astype(F32)
        if split:
            rows = R // G
            for j in range(G):
                tot[p][j] = total[j * rows : (j + 1) * rows]
                zs[p][j] = total[j * rows : (j + 1) * rows].astype(BF16)
        else:
            zs[p][...] = total.astype(BF16)
        for copy in z_copies(p):
            copy.start()

    def stage3(p):
        z_all(p).wait_recv()
        if split:
            total = tot[p][g]
            for k in range(G - 1):
                total = total + zr[p][k].astype(F32)
            ag[p][g] = total.astype(BF16)
            for copy in a_copies(p):
                copy.start()
        else:
            for k in range(G - 1):
                ag[p][lax.rem(g + G - k - 1, G)] = zr[p][k]
            ag[p][g] = zs[p][...]
            total = ag[p][0].astype(F32)
            for k in range(1, G):
                total = total + ag[p][k].astype(F32)
            put(p, total)

    def stage4(p):
        if not split:
            return
        a_all(p).wait_recv()
        put(p, jnp.concatenate([ag[p][j].astype(F32) for j in range(G)], axis=0))

    stores = [
        pltpu.make_async_copy(src, dst, out_sem.at[k])
        for k, (src, dst) in enumerate(zip((block_ref, gin_ref, taps_ref, gb_ref, gout_ref), results))
    ]

    def sent(p):
        x_all(p).wait_send()

    stage0(0)
    if NP > 1:
        stage0(1)
    stage1(0)
    for p in range(2, NP):
        stage0(p)
    tap_s[...] = dot(gp[...], wt_ref[:width, :], ((1,), (1,))).astype(BF16)
    block_ref[...] = (sig_ref[...].astype(F32) + dot(hid[...], wo_ref[...])).astype(BF16)
    stores[0].start()
    near[...] = cot_ref[...].astype(F32) + dot(gp[...], wt_ref[width:, :], ((1,), (1,)))
    for step in range(1, NP + 3):
        if step < NP:
            sent(step - 1)
            stage1(step)
        if step == NP:
            sent(NP - 1)

            @pl.when(has_prev)
            def _():
                back.start()

        if step - 1 < NP:
            stage2(step - 1)
        if 0 <= step - 2 < NP:
            stage3(step - 2)
        if 0 <= step - 3 < NP:
            stage4(step - 3)

    @pl.when(has_next)
    def _():
        back.wait_recv()

    @pl.when(jnp.logical_not(has_next))
    def _():
        tap_r[...] = jnp.zeros_like(tap_r)

    gin_ref[...] = (near[...] + tap_r[...].astype(F32)).astype(BF16)
    for store in stores[1:]:
        store.start()

    @pl.when(has_next)
    def _():
        halo.wait_send()

    @pl.when(has_prev)
    def _():
        back.wait_send()

    for p in range(NP):
        core_copy(p).wait_send()
        z_all(p).wait_send()
        if split:
            a_all(p).wait_send()
    for store in stores:
        store.wait()


def write_out(*refs):
    ins, outs, sem = refs[:5], refs[5:10], refs[10]
    copies = [pltpu.make_async_copy(ins[k], outs[k], sem.at[k]) for k in range(5)]
    for copy in copies:
        copy.start()
    for copy in copies:
        copy.wait()


def per_device(S, G, signal, cotangent, w_taps, gate_bias, w_out):
    steps, width = signal.shape
    units = w_out.shape[0]
    C = S // 2
    R = 2 * width // S
    U = UNIT_BLOCK
    NB = units // U
    sizes = [2 * U] * NB + [width + BIAS_LANES]
    pieces = []
    for members in LAYOUT[NB, GROUPS]:
        placed, at = [], 0
        for block in members:
            placed.append((block, at))
            at += sizes[block]
        pieces.append((tuple(placed), at))
    widths = [w for _, w in pieces]
    NP = len(pieces)
    split = R % (16 * G) == 0
    share = 2 * units // S
    zrows = R // G if split else R
    V = pltpu.VMEM
    D = pltpu.SemaphoreType.DMA
    scratch = [
        V((steps, width), BF16),
        V((steps, width), BF16),
        V((2 * width, 2 * units), BF16),
        V((1, 2 * units), F32),
        V((units, width), BF16),
        D((5,)),
        V((steps, width), BF16),
        V((steps, width), BF16),
        V((R, 2 * units), F32),
        V((1, share), F32),
        V((units // S, width), F32),
        D((5,)),
        V((steps, width), F32),
        V((steps, width), BF16),
        V((steps, 2 * units), F32),
        V((steps, units), F32),
        V((steps, 2 * units), BF16),
        V((steps, units), BF16),
        V((steps, width), BF16),
        V((steps, width), BF16),
    ]
    scratch += [V((2, C, R, w), F32) for w in widths]
    scratch += [V((C, R, w), F32) for w in widths]
    scratch += [V((C - 1, R, w), BF16) for w in widths]
    scratch += [V((C - 1, R, w), BF16) for w in widths]
    scratch += [V((G, zrows, w) if split else (8, 128), F32) for w in widths]
    scratch += [V((G, zrows, w) if split else (zrows, w), BF16) for w in widths]
    scratch += [V((G - 1, zrows, w), BF16) for w in widths]
    scratch += [V((G, zrows, w), BF16) for w in widths]
    scratch += [D((2,)), D((2,))] + [D((NP,)) for _ in range(8)]
    vmem = pl.BlockSpec(memory_space=pltpu.VMEM)
    outs = pl.pallas_call(
        functools.partial(kernel, (S, G, C, R, tuple(pieces), split)),
        out_shape=(
            jax.ShapeDtypeStruct((steps, width), BF16),
            jax.ShapeDtypeStruct((steps, width), BF16),
            jax.ShapeDtypeStruct((R, 2 * units), F32),
            jax.ShapeDtypeStruct((1, share), F32),
            jax.ShapeDtypeStruct((units // S, width), F32),
        ),
        in_specs=[pl.BlockSpec(memory_space=pltpu.HBM)] * 5,
        out_specs=[pl.BlockSpec(memory_space=pltpu.HBM)] * 5,
        scratch_shapes=scratch,
        compiler_params=pltpu.CompilerParams(
            collective_id=0, has_side_effects=True, vmem_limit_bytes=64000 * 1024
        ),
        cost_estimate=pl.CostEstimate(
            flops=2 * steps * width * units * 16, bytes_accessed=4 << 20, transcendentals=2 * steps * units
        ),
    )(signal, cotangent, w_taps, gate_bias.reshape(1, -1), w_out)
    block_out, grad_in, grad_taps, grad_bias, grad_out = pl.pallas_call(
        write_out,
        out_shape=tuple(jax.ShapeDtypeStruct(o.shape, o.dtype) for o in outs),
        in_specs=[vmem] * 5,
        out_specs=[pl.BlockSpec(memory_space=pltpu.HBM)] * 5,
        scratch_shapes=[D((5,))],
    )(*outs)
    grad_bias = grad_bias.reshape(-1)
    return block_out, grad_in, grad_taps, grad_bias, grad_out


def solution(mesh):
    S, G = mesh.shape["seq"], mesh.shape["grp"]
    rows = P(("grp", "seq"), None)
    return jax.shard_map(
        functools.partial(per_device, S, G),
        mesh=mesh,
        in_specs=(rows, rows, P(), P(), P()),
        out_specs=(rows, rows, P("seq", None), P("seq"), P("seq", None)),
        check_vma=False,
    )
```

time: 36.5 us -> 36.4 us (level)
  no operation moved by 1% of the time
where the time goes in v3:
time: 36.4 us; the launch traced here: 36.3 us
  Pallas kernels  35.6 us (98%)
  between operations  0.64 us (2%)
    pallas_call x1, Pallas kernels, per_device(): pl.pallas_call(functools.partial(kernel, (S, G, C, R, tuple(pieces), spli...  33.7 us
    pallas_call x1, Pallas kernels, per_device(): pl.pallas_call(write_out, out_shape=tuple((jax.ShapeDtypeStruct(o.shape,...  1.94 us

profile of v3, /device:TPU:0, one launch (start us, length us, event | category | flops | bytes accessed | tf_op | source)
XLA Modules:
  0.0 36.3 jit_solution(5014878770542292653)
XLA Ops:
  0.6 33.7 %shard_map.92 = (bf16[256,256]{1,0:T(8,128)(2,1)}, bf16[256,256]{1,0:T(8,128)(2,1)}, f32[64,1024]{1,0:T(8,128)}, f32[1,128]{1,0:T(1,128)}, f32[64,256]{1,0:T(8,128)}) custom-call(bf16[256,256]{1,0:T(8,128)(2,1)} %sig_in.1, bf16[256,256]{1,0:T(8,128)(2,1)} %cot_in.1, bf16[512,1024]{1,0:T(8,128)(2,1)} %wt_in.1, f32[1,1024]{1,0:T(1,128)} %bitcast.2, ...), custom_call_target="tpu_custom_call" | custom-call | flops 1073741824 | bytes 4194304 | tf_op jit(solution)/shard_map/pallas_call | solution.py:358
  34.3 1.9 %shard_map.93 = (bf16[256,256]{1,0:T(8,128)(2,1)}, bf16[256,256]{1,0:T(8,128)(2,1)}, f32[64,1024]{1,0:T(8,128)}, f32[1,128]{1,0:T(1,128)}, f32[64,256]{1,0:T(8,128)}) custom-call(bf16[256,256]{1,0:T(8,128)(2,1)} %get-tuple-element.15.refs_0_, bf16[256,256]{1,0:T(8,128)(2,1)} %get-tuple-element.16.refs_1_, f32[64,1024]{1,0:T(8,128)} %get-tuple-element.17.refs_2_, ...), custom_call_target="tpu_custom_call" | custom-call | tf_op jit(solution)/shard_map/pallas_call | solution.py:377
